TPU v7x, 32 devices: a whole 2x2x4 slice. The times are simulated.
32 devices in a mesh: days: 2 (over y), blk: 4 (over z), det: 2 (over x), beam: 2 (over core).
Axes of the slice: x: 2, y: 2, z: 4, core: 2. Of those that a mesh axis runs over, the one named last changes fastest.
Arguments:
- solution: float32 [2, 264, 2048], P(None, ('days', 'blk'), 'det'), parts along dimension 1, may hold values from -6 to 6
- residual: float32 [2, 264, 2048], P(None, ('days', 'blk'), 'det'), parts along dimension 1, may hold values from -6 to 6
- direction: float32 [2, 264, 2048], P(None, ('days', 'blk'), 'det'), parts along dimension 1, may hold values from -6 to 6
- legendre: bfloat16 [132, 2048, 4], P('blk', 'det'), may hold values from -0.125 to 0.125
- beam_coef: float32 [2048, 16], P('det', 'beam'), may hold values from 0.5 to 1.5
- prior_weight: float32 [2048], P('det'), may hold values from 1 to 16
- tile_ids: int32 [16, 32], P(('days', 'blk', 'det')), parts along dimension 0, may hold values from 0 to 63, as said below
- interp_weight: bfloat16 [16, 32, 128, 128], P(('days', 'blk', 'det')), parts along dimension 0, may hold values from -0.5 to 0.5
- psi_angle: float32 [16, 32, 128], P(('days', 'blk', 'det')), parts along dimension 0, may hold values from -3.140625 to 3.140625
- noise_coef: float32 [16, 4, 8], P(('days', 'blk', 'det')), parts along dimension 0, may hold values from -0.3 to 0.3
- band_width: int32 [16, 4], P(('days', 'blk', 'det')), parts along dimension 0, may hold values from 1 to 8
Outputs:
- new_solution: float32 [2, 264, 2048], P(None, ('days', 'blk'), 'det'), parts along dimension 1
- new_residual: float32 [2, 264, 2048], P(None, ('days', 'blk'), 'det'), parts along dimension 1
- new_direction: float32 [2, 264, 2048], P(None, ('days', 'blk'), 'det'), parts along dimension 1
There are 2 independent parts, one for each index of `days`. A program takes and returns all parts, laid end to end along the dimension named above; an argument that names none is the same for every part. Nothing has to cross between parts.
Inputs may be any that keep to these rules, and one draw needn't show every extreme that they name: `tile_ids`: tile g lies on cycle g // 16; in every span at most 16 visits read tiles of one cycle, and exactly 16 for some cycle.
All inputs are finite; a program needn't handle non-finite values.
Results may differ from a plain program's by a relative error of at most 0.0024.
Values may be sent and summed in bfloat16 or wider, within the bound.
A program may use at most 64 MiB of HBM per device.

v0:
```python
import math

import jax
import jax.numpy as jnp
from jax import lax
from jax.sharding import PartitionSpec as P

K = 16
P_SIZE = 2048
TPIX = 128
SPD = 1024
BW = 8


def beam_basis(angles, mode_ids):
    half_modes = K // 2
    orders = jnp.where(mode_ids < half_modes, mode_ids, mode_ids - half_modes + 1).astype(
        jnp.float32
    )
    phases = angles[..., None, :] * orders[:, None]
    return jnp.where((mode_ids < half_modes)[:, None], jnp.cos(phases), jnp.sin(phases))


def fourier_table(orders_total, col_start, col_count):
    order_idx = jnp.arange(orders_total, dtype=jnp.int32)
    pixel_idx = col_start + jnp.arange(col_count, dtype=jnp.int32)
    phase = (order_idx[:, None] * pixel_idx[None, :] % P_SIZE).astype(jnp.float32) * (
        2.0 * math.pi / P_SIZE
    )
    norm_scale = 1.0 / math.sqrt(2.0 * orders_total)
    return (jnp.concatenate([jnp.cos(phase), -jnp.sin(phase)], 0) * norm_scale).astype(jnp.bfloat16)


def noise_apply(samples, coefficients, widths):
    lag_ids = jnp.arange(1, BW + 1, dtype=jnp.int32)
    active = (lag_ids <= widths[..., None]).astype(jnp.float32)
    tap_coef = coefficients * active
    center = 1.0 + 2.0 * jnp.sum(jnp.abs(tap_coef), axis=-1)
    padding = ((0, 0),) * (samples.ndim - 1) + ((BW, BW),)
    padded = jnp.pad(samples, padding)
    filtered_sum = center[..., None] * samples
    for lag_step in range(1, BW + 1):
        before = padded[..., BW - lag_step : BW - lag_step + SPD]
        after = padded[..., BW + lag_step : BW + lag_step + SPD]
        filtered_sum = filtered_sum + tap_coef[..., lag_step - 1 : lag_step] * (before + after)
    return filtered_sum


def send_requests(request_table):
    return lax.all_to_all(request_table, "blk", split_axis=0, concat_axis=0, tiled=True)


def body(
    solution,
    residual,
    direction,
    legendre,
    beam_coef,
    prior_weight,
    tile_ids,
    interp_weight,
    psi_angle,
    noise_coef,
    band_width,
):
    blocks = lax.axis_size("blk")
    mode_count = beam_coef.shape[1]
    mode_ids = lax.axis_index("beam") * mode_count + jnp.arange(mode_count, dtype=jnp.int32)
    beam_rows = jnp.transpose(beam_coef)[None, :, None, :]
    scaled = (direction[:, None, :, :] * beam_rows).astype(jnp.bfloat16)
    partial_value = jnp.einsum(
        "ckml,mlr->ckmr", scaled, legendre, preferred_element_type=jnp.float32
    ).astype(jnp.bfloat16)
    gathered = lax.all_to_all(partial_value, "blk", split_axis=3, concat_axis=2, tiled=True)
    coeffs = lax.psum(gathered.astype(jnp.float32).astype(jnp.bfloat16), "det")
    orders_total = coeffs.shape[2]
    cycle_coeffs = jnp.transpose(coeffs[:, :, :, 0], (1, 0, 2)).reshape(
        mode_count, 2 * orders_total
    )
    block_width = min(P_SIZE, 512)
    table_blocks = [
        fourier_table(orders_total, col_start, block_width)
        for col_start in range(0, P_SIZE, block_width)
    ]
    pieces = [
        jnp.dot(cycle_coeffs, table_block, preferred_element_type=jnp.float32)
        for table_block in table_blocks
    ]
    cycle_cube = jnp.concatenate(pieces, 1).astype(jnp.bfloat16)
    tile_count = P_SIZE // TPIX
    cycle_tiles = cycle_cube.reshape(mode_count, tile_count, TPIX)
    slot_ids = tile_ids[0]
    slot_count = slot_ids.shape[0]
    capacity = 2 * slot_count // blocks
    owners = slot_ids // tile_count
    local_ids = slot_ids % tile_count
    owner_hot = (owners[:, None] == jnp.arange(blocks, dtype=jnp.int32)[None, :]).astype(jnp.int32)
    earlier = jnp.cumsum(owner_hot, axis=0) - owner_hot
    slot_ranks = jnp.sum(earlier * owner_hot, axis=1)
    positions = owners * capacity + slot_ranks
    request_table = (
        jnp.full((blocks * capacity,), -1, jnp.int32)
        .at[positions]
        .set(local_ids)
        .reshape(blocks, capacity)
    )
    incoming = None
    every_tile = lax.all_gather(cycle_tiles, "blk", axis=1, tiled=True)
    slot_tiles = jnp.take(every_tile, slot_ids, axis=1)
    weights = interp_weight[0]
    values = jnp.einsum("stp,ksp->skt", weights, slot_tiles, preferred_element_type=jnp.float32)
    mode_basis = beam_basis(psi_angle[0], mode_ids)
    signal = lax.psum(jnp.sum(mode_basis * values, axis=1), "beam")
    filtered = noise_apply(signal.reshape(-1, SPD), noise_coef[0], band_width[0]).reshape(
        signal.shape
    )
    weighted = (mode_basis * filtered[:, None, :]).astype(jnp.bfloat16)
    slot_adj = jnp.einsum("skt,stp->skp", weighted, weights, preferred_element_type=jnp.float32)
    incoming = send_requests(request_table)
    outgoing = (
        jnp.zeros((blocks * capacity, mode_count, TPIX), jnp.float32).at[positions].set(slot_adj)
    )
    outgoing = outgoing.reshape(blocks, capacity, mode_count, TPIX)
    returned = lax.all_to_all(outgoing, "blk", split_axis=0, concat_axis=0, tiled=True)
    owner_match = (
        incoming.reshape(-1)[:, None] == jnp.arange(tile_count, dtype=jnp.int32)[None, :]
    ).astype(jnp.float32)
    tile_part = jnp.einsum(
        "nt,nkp->ktp",
        owner_match,
        returned.reshape(-1, mode_count, TPIX),
        precision=lax.Precision.HIGHEST,
    )
    tile_total = lax.psum(tile_part, "det")
    cycle_adj = tile_total.reshape(mode_count, P_SIZE).astype(jnp.bfloat16)
    back_total = jnp.zeros((mode_count, 2 * orders_total), jnp.float32)
    for block_index, table_block in enumerate(table_blocks):
        col_start = block_index * block_width
        back_total = back_total + jnp.einsum(
            "kp,np->kn",
            cycle_adj[:, col_start : col_start + block_width],
            table_block,
            preferred_element_type=jnp.float32,
        )
    back_coef = back_total.astype(jnp.bfloat16).reshape(mode_count, 2, orders_total)
    back_coef = jnp.transpose(back_coef, (1, 0, 2))[:, :, :, None]
    returned_coef = lax.all_to_all(back_coef, "blk", split_axis=2, concat_axis=3, tiled=True)
    spread = jnp.einsum(
        "ckmr,mlr->ckml", returned_coef, legendre, preferred_element_type=jnp.float32
    )
    image_part = jnp.sum(spread * beam_rows, axis=1)
    image_field = lax.psum(image_part, "beam") + prior_weight[None, None, :] * direction
    old_norm = lax.psum(jnp.sum(residual * residual), ("blk", "det"))
    curvature = lax.psum(jnp.sum(direction * image_field), ("blk", "det"))
    step_alpha = old_norm / curvature
    new_solution = solution + step_alpha * direction
    new_residual = residual - step_alpha * image_field
    new_norm = lax.psum(jnp.sum(new_residual * new_residual), ("blk", "det"))
    new_direction = new_residual + new_norm / old_norm * direction
    return (new_solution, new_residual, new_direction)


def solution(mesh):
    in_specs = (
        P(None, ("days", "blk"), "det"),
        P(None, ("days", "blk"), "det"),
        P(None, ("days", "blk"), "det"),
        P("blk", "det", None),
        P("det", "beam"),
        P("det"),
        P(("days", "blk", "det"), None),
        P(("days", "blk", "det"), None, None, None),
        P(("days", "blk", "det"), None, None),
        P(("days", "blk", "det"), None, None),
        P(("days", "blk", "det"), None),
    )
    out_specs = (
        P(None, ("days", "blk"), "det"),
        P(None, ("days", "blk"), "det"),
        P(None, ("days", "blk"), "det"),
    )
    return jax.shard_map(body, mesh=mesh, in_specs=in_specs, out_specs=out_specs, check_vma=False)
```

profile of v0, /device:TPU:0, one launch (start us, length us, event | category | flops | bytes accessed | tf_op | source)
XLA Modules:
  0.0 163.8 jit_solution(3671773575160134356)
XLA Ops:
  7.2 3.6 %fusion.1 = bf16[2,8,33,4]{1,3,0,2:T(4,128)(2,1)S(1)} fusion(f32[8,1024]{1,0:T(8,128)} %bitcast.152, f32[2,33,1024]{2,0,1:T(2,128)} %param.13, bf16[33,1024,4]{1,2,0:T(4,128)(2,1)} %param.14), kind=kOutput, calls=%fused_computation.8 | convolution fusion | flops 5408832 | bytes 577664 | tf_op jit(solution)/shard_map/ckml,mlr->ckmr/dot_general | solution.py:71
  11.0 0.7 reshape.250
  11.7 6.3 %all-to-all-start = ((bf16[4,2,264]{2,1,0:T(2,128)(2,1)}), bf16[4,2,264]{2,1,0:T(2,128)(2,1)S(1)}, u32[]{:S(2)}, u32[]{:S(2)}) async-start(bf16[4,2,264]{2,1,0:T(2,128)(2,1)} %reshape.250), calls=%async_computation | async-start | bytes 12288 | tf_op jit(solution)/shard_map/all_to_all | solution.py:74
  18.0 1.1 sine_negate_fusion.3
  19.2 1.1 fusion.48
  20.3 1.1 fusion.49
  21.4 1.1 fusion.47
  23.4 0.7 scatter_custom_fusion.1
  24.1 0.7 all_to_all.40
  24.7 5.1 %all-to-all-start.2 = ((s32[4,1,16]{2,1,0:T(1,128)}), s32[4,1,16]{2,1,0:T(1,128)S(1)}, u32[]{:S(2)}, u32[]{:S(2)}) async-start(s32[4,1,16]{2,1,0:T(1,128)} %bitcast.24), calls=%async_computation.2 | async-start | bytes 4096 | tf_op jit(solution)/shard_map/all_to_all | solution.py:50
  30.1 5.0 %psum.50 = bf16[8,264]{1,0:T(8,128)(2,1)S(1)} all-reduce(bf16[8,264]{1,0:T(8,128)(2,1)S(1)} %reshape.198), channel_id=1, replica_groups=mesh['days'=2,'blk'=4,'det'=2,'beam'=2] {'det'}, use_global_device_ids=true, to_apply=%region_5.6 | all-reduce | flops 2112 | bytes 8448 | tf_op jit(solution)/shard_map/psum | solution.py:75
  35.8 14.0 %all_gather.3 = bf16[8,64,128]{2,0,1:T(8,128)(2,1)S(1)} all-gather(bf16[8,16,128]{2,0,1:T(8,128)(2,1)S(1)} %pad_maximum_fusion), channel_id=1, replica_groups=mesh['days'=2,'blk'=4,'det'=2,'beam'=2] {'blk'}, dimensions={1}, use_global_device_ids=true | all-gather | bytes 163840 | tf_op jit(solution)/shard_map/all_gather | solution.py:108
  49.8 0.6 gather_fusion
  50.5 0.7 fusion
  51.2 3.4 %psum.51 = f32[4,1024]{1,0:T(4,128)S(1)} all-reduce(f32[4,1024]{1,0:T(4,128)S(1)} %reshape.199), channel_id=1, replica_groups=mesh['days'=2,'blk'=4,'det'=2,'beam'=2] {'beam'}, use_global_device_ids=true, to_apply=%region_7.8 | all-reduce | flops 4096 | bytes 32768 | tf_op jit(solution)/shard_map/psum | solution.py:113
  54.8 1.3 fusion.5
  56.1 2.6 %scatter_fusion = f32[64,8,128]{2,1,0:T(8,128)S(1)} fusion(f32[64,8,128]{2,1,0:T(8,128)S(1)} %broadcast_in_dim.21, s32[32]{0:T(128)S(1)} %get-tuple-element.28, f32[32,8,128]{2,1,0:T(8,128)} %fusion.5), kind=kCustom, calls=%fused_computation.1 | custom fusion | bytes 393344 | tf_op jit(solution)/shard_map/scatter | solution.py:121
  58.7 0.8 copy.35
  59.5 4.5 %all-to-all-start.1 = ((f32[4,16,8,128]{3,1,2,0:T(8,128)}), f32[4,16,8,128]{3,1,2,0:T(8,128)S(1)}, u32[]{:S(2)}, u32[]{:S(2)}) async-start(f32[4,16,8,128]{3,1,2,0:T(8,128)} %copy.35), calls=%async_computation.1 | async-start | bytes 524288 | tf_op jit(solution)/shard_map/all_to_all | solution.py:124
  64.0 0.5 broadcast.339
  64.5 0.7 reduce.20
  65.2 8.1 %all-to-all-done.1 = f32[4,16,8,128]{3,1,2,0:T(8,128)S(1)} async-done(((f32[4,16,8,128]{3,1,2,0:T(8,128)}), f32[4,16,8,128]{3,1,2,0:T(8,128)S(1)}, u32[]{:S(2)}, u32[]{:S(2)}) %all-to-all-start.1) | async-done | bytes 262176 | tf_op jit(solution)/shard_map/all_to_all | solution.py:124
  73.6 8.9 %psum.52 = bf16[8,16,128]{2,1,0:T(8,128)(2,1)S(1)} all-reduce(f32[8,16,128]{2,1,0:T(8,128)S(1)} %convolution_bitcast_fusion), channel_id=1, replica_groups=mesh['days'=2,'blk'=4,'det'=2,'beam'=2] {'det'}, use_global_device_ids=true, to_apply=%region_10.11 | all-reduce | flops 16384 | bytes 98304 | tf_op jit(solution)/shard_map/psum | solution.py:134
  83.7 8.2 %all_to_all.50 = bf16[4,2,264]{2,1,0:T(2,128)(2,1)S(1)} all-to-all(bf16[4,2,264]{2,1,0:T(2,128)(2,1)S(1)} %reshape.252), channel_id=1, replica_groups=mesh['days'=2,'blk'=4,'det'=2,'beam'=2] {'blk'}, dimensions={0} | all-to-all | bytes 8448 | tf_op jit(solution)/shard_map/all_to_all | solution.py:147
  92.0 1.7 %multiply_reduce_fusion = f32[33,2,1024]{2,1,0:T(2,128)} fusion(f32[8,1024]{1,0:T(8,128)S(1)} %bitcast.153, bf16[33,1024,4]{1,2,0:T(4,128)(2,1)S(1)} %copy-done.10, bf16[2,8,4,33,1]{1,0,3,2,4:T(2,128)(2,1)S(1)} %bitcast.146), kind=kOutput, calls=%fused_computation.3 | convolution fusion | flops 5339136 | bytes 577664 | tf_op jit(solution)/shard_map/ckmr,mlr->ckml/dot_general | solution.py:148
  93.7 0.9 multiply_reduce_fusion.3
  94.6 14.9 %all-reduce.4.cloned.1.call-done = f32[2,33,1024]{2,0,1:T(2,128)} async-done(((f32[2,33,1024]{2,0,1:T(2,128)}), f32[2,33,1024]{2,0,1:T(2,128)}) %all-reduce.4.cloned.1.call-update) | async-done | bytes 270352 | tf_op jit(solution)/shard_map/psum | solution.py:152
  109.4 1.8 %multiply_reduce_fusion.2 = f32[]{:T(128)} fusion(f32[2,33,1024]{2,0,1:T(2,128)S(1)} %copy-done.1, f32[2,33,1024]{2,0,1:T(2,128)} %all-reduce.4.cloned.1.call-done, f32[1024]{0:T(1024)S(1)} %copy-done.6), kind=kLoop, calls=%fused_computation.85 | loop fusion | flops 270335 | bytes 544772 | tf_op jit(solution)/shard_map/reduce_sum | solution.py:154
  111.3 22.3 %all-reduce.1 = (f32[]{:T(128)}, f32[]{:T(128)}) all-reduce(f32[]{:T(128)} %multiply_reduce_fusion.3, f32[]{:T(128)} %multiply_reduce_fusion.2), channel_id=1, replica_groups=mesh['days'=2,'blk'=4,'det'=2,'beam'=2] {'blk','det'}, use_global_device_ids=true, to_apply=%region_1.2 | all-reduce | flops 2 | bytes 16 | tf_op jit(solution)/shard_map/psum | solution.py:153
  134.9 1.9 %multiply_reduce_fusion.1 = (f32[]{:T(128)}, f32[2,33,1024]{2,0,1:T(2,128)S(1)}) fusion(f32[2,33,1024]{2,0,1:T(2,128)S(1)} %copy-done.2, f32[2,33,1024]{2,0,1:T(2,128)} %all-reduce.4.cloned.1.call-done, f32[2,33,1024]{2,0,1:T(2,128)S(1)} %copy-done.1, f32[1024]{0:T(1024)S(1)} %copy-done.6, f32[]{:T(128)S(6)} %div.34), kind=kLoop, calls=%fused_computation.82 | loop fusion | flops 405503 | bytes 1085448 | tf_op jit(solution)/shard_map/reduce_sum | solution.py:158
  136.8 17.7 %psum.55 = f32[]{:T(128)} all-reduce(f32[]{:T(128)} %get-tuple-element.13), channel_id=1, replica_groups=mesh['days'=2,'blk'=4,'det'=2,'beam'=2] {'blk','det'}, use_global_device_ids=true, to_apply=%region_16.17 | all-reduce | flops 1 | bytes 8 | tf_op jit(solution)/shard_map/psum | solution.py:158
  155.8 1.1 multiply_add_fusion
  (73 shorter events, 3.9 us)
Async XLA Ops:
  7.2 43.3 %copy-start = (bf16[1,32,128,128]{3,2,1,0:T(8,128)(2,1)S(1)}, bf16[1,32,128,128]{3,2,1,0:T(8,128)(2,1)}, u32[]{:S(2)}) copy-start(bf16[1,32,128,128]{3,2,1,0:T(8,128)(2,1)} %param.18) | copy-start | bytes 3145732
  7.2 11.9 %copy-start.8 = (s32[1,32]{1,0:T(1,128)S(1)}, s32[1,32]{1,0:T(1,128)}, u32[]{:S(2)}) copy-start(s32[1,32]{1,0:T(1,128)} %param.17) | copy-start | bytes 388
  11.7 13.1 %all-to-all-start = ((bf16[4,2,264]{2,1,0:T(2,128)(2,1)}), bf16[4,2,264]{2,1,0:T(2,128)(2,1)S(1)}, u32[]{:S(2)}, u32[]{:S(2)}) async-start(bf16[4,2,264]{2,1,0:T(2,128)(2,1)} %reshape.250), calls=%async_computation | async-start | bytes 12288 | tf_op jit(solution)/shard_map/all_to_all | solution.py:74
  18.0 4.9 %copy-start.7 = (f32[1,4,8]{2,1,0:T(4,128)S(1)}, f32[1,4,8]{2,1,0:T(4,128)}, u32[]{:S(2)}) copy-start(f32[1,4,8]{2,1,0:T(4,128)} %param.20) | copy-start | bytes 388
  18.0 4.9 %copy-start.9 = (s32[1,4]{1,0:T(1,128)S(1)}, s32[1,4]{1,0:T(1,128)}, u32[]{:S(2)}) copy-start(s32[1,4]{1,0:T(1,128)} %param.21) | copy-start | bytes 52
  24.7 34.7 %all-to-all-start.2 = ((s32[4,1,16]{2,1,0:T(1,128)}), s32[4,1,16]{2,1,0:T(1,128)S(1)}, u32[]{:S(2)}, u32[]{:S(2)}) async-start(s32[4,1,16]{2,1,0:T(1,128)} %bitcast.24), calls=%async_computation.2 | async-start | bytes 4096 | tf_op jit(solution)/shard_map/all_to_all | solution.py:50
  35.3 15.2 %copy-start.5 = (f32[1,32,128]{2,1,0:T(8,128)S(1)}, f32[1,32,128]{2,1,0:T(8,128)}, u32[]{:S(2)}) copy-start(f32[1,32,128]{2,1,0:T(8,128)} %param.19) | copy-start | bytes 49156
  59.5 13.9 %all-to-all-start.1 = ((f32[4,16,8,128]{3,1,2,0:T(8,128)}), f32[4,16,8,128]{3,1,2,0:T(8,128)S(1)}, u32[]{:S(2)}, u32[]{:S(2)}) async-start(f32[4,16,8,128]{3,1,2,0:T(8,128)} %copy.35), calls=%async_computation.1 | async-start | bytes 524288 | tf_op jit(solution)/shard_map/all_to_all | solution.py:124
  64.0 45.5 %all-reduce.4.cloned.1.call-start = ((), (), s32[]{:S(2)}) async-start(), calls=%async_computation.4 | async-start | bytes 540672 | tf_op jit(solution)/shard_map/psum | solution.py:152
  82.7 9.3 %copy-start.10 = (bf16[33,1024,4]{1,2,0:T(4,128)(2,1)S(1)}, bf16[33,1024,4]{1,2,0:T(4,128)(2,1)}, u32[]{:S(2)}) copy-start(bf16[33,1024,4]{1,2,0:T(4,128)(2,1)} %param.14) | copy-start | bytes 811012
  82.9 9.1 %copy-start.11 = (f32[1024,8]{0,1:T(8,128)S(1)}, f32[1024,8]{0,1:T(8,128)}, u32[]{:S(2)}) copy-start(f32[1024,8]{0,1:T(8,128)} %param.15) | copy-start | bytes 98308
  83.3 10.4 %copy-start.2 = (f32[2,33,1024]{2,0,1:T(2,128)S(1)}, f32[2,33,1024]{2,0,1:T(2,128)}, u32[]{:S(2)}) copy-start(f32[2,33,1024]{2,0,1:T(2,128)} %param.12) | copy-start | bytes 811012
  91.8 17.6 %copy-start.1 = (f32[2,33,1024]{2,0,1:T(2,128)S(1)}, f32[2,33,1024]{2,0,1:T(2,128)}, u32[]{:S(2)}) copy-start(f32[2,33,1024]{2,0,1:T(2,128)} %param.13) | copy-start | bytes 811012
  91.8 17.6 %copy-start.6 = (f32[1024]{0:T(1024)S(1)}, f32[1024]{0:T(1024)}, u32[]{:S(2)}) copy-start(f32[1024]{0:T(1024)} %param.16) | copy-start | bytes 12292
  93.7 62.2 %copy-start.4 = (f32[2,33,1024]{2,0,1:T(2,128)S(1)}, f32[2,33,1024]{2,0,1:T(2,128)}, u32[]{:S(2)}) copy-start(f32[2,33,1024]{2,0,1:T(2,128)} %param.11) | copy-start | bytes 811012
  136.7 20.2 %copy-start.3 = (f32[2,33,1024]{2,0,1:T(2,128)}, f32[2,33,1024]{2,0,1:T(2,128)S(1)}, u32[]{:S(2)}) copy-start(f32[2,33,1024]{2,0,1:T(2,128)S(1)} %get-tuple-element.14) | copy-start | bytes 811012
Sparse Core Ops, SparseCore 0:
  93.8 15.5 all-reduce.3
where the time goes:
time: 164 us
  blocking collectives  79.4 us (48%)
  waiting for transfers between devices  23 us (14%)
  between operations  17 us (10%)
  starting transfers between devices  15.9 us (10%)
  other arithmetic  11.5 us (7%)
  matrix products  9 us (5%)
  local copies, waits for them, and re-layouts  7.95 us (5%)
    psum x1, blocking collectives, body(): old_norm = lax.psum(jnp.sum(residual * residual), ('blk', 'det'))  22.3 us
    psum x1, blocking collectives, body(): new_norm = lax.psum(jnp.sum(new_residual * new_residual), ('blk', 'det'))  17.7 us
    psum x1, waiting for transfers between devices, body(): lax.psum(image_part, 'beam') + prior_weight[None, None, :] * direction  14.9 us
    all_gather x1, blocking collectives, body(): every_tile = lax.all_gather(cycle_tiles, 'blk', axis=1, tiled=True)  14 us
    psum x1, blocking collectives, body(): tile_total = lax.psum(tile_part, 'det')  8.88 us
    all_to_all x1, blocking collectives, body(): lax.all_to_all(back_coef, 'blk', split_axis=2, concat_axis=3, tiled=True)  8.15 us
    all_to_all x1, waiting for transfers between devices, body(): lax.all_to_all(outgoing, 'blk', split_axis=0, concat_axis=0, tiled=True)  8.12 us
    all_to_all x1, starting transfers between devices, body(): lax.all_to_all(partial_value, 'blk', split_axis=3, concat_axis=2, tiled=T...  6.32 us
  transfers between devices with their start and end apart: 4, of which 2 were waited for; matrix products, arithmetic and copies ran while one was open for 9% of the time, Pallas kernels for 0%

commit v1 on v0

v1 whole, which is shorter than its diff:
```python
import functools
import math

import jax
import jax.numpy as jnp
import ml_dtypes
import numpy as np
from jax import lax
from jax.experimental import pallas as pl
from jax.experimental.pallas import tpu as pltpu
from jax.sharding import PartitionSpec as P

K = 16
P_SIZE = 2048
TPIX = 128
SPD = 1024
BW = 8
LANES = 128
HALF = 64
F32 = jnp.float32
BF16 = jnp.bfloat16
MESH = pl.DeviceIdType.MESH


def padded_table(blocks, orders):
    total = blocks * orders
    m = np.arange(total, dtype=np.int64)
    j = np.arange(P_SIZE, dtype=np.int64)
    phase = ((m[:, None] * j[None, :]) % P_SIZE).astype(np.float32) * np.float32(
        2.0 * math.pi / P_SIZE
    )
    scale = np.float32(1.0 / math.sqrt(2.0 * total))
    table = np.zeros((blocks, 2, HALF, P_SIZE), np.float32)
    table[:, 0, :orders] = (np.cos(phase) * scale).reshape(blocks, orders, P_SIZE)
    table[:, 1, :orders] = (-np.sin(phase) * scale).reshape(blocks, orders, P_SIZE)
    return table.reshape(blocks * LANES, P_SIZE).astype(ml_dtypes.bfloat16)


def loop(count, step):
    if count <= 8:
        for i in range(count):
            step(i)
    else:
        lax.fori_loop(0, count, lambda i, c: (step(i), c)[1], 0)


def mult(x, m):
    return x if isinstance(x, int) else pl.multiple_of(x, m)


def dot_nt(a, b):
    return lax.dot_general(a, b, (((1,), (1,)), ((), ())), preferred_element_type=F32)


def dot_nn(a, b):
    return lax.dot_general(a, b, (((1,), (0,)), ((), ())), preferred_element_type=F32)


def dot_tn(a, b):
    return lax.dot_general(a, b, (((0,), (0,)), ((), ())), preferred_element_type=F32)


def split2(x):
    hi = x.astype(BF16)
    return hi, (x - hi.astype(F32)).astype(BF16)


def kernel(
    nb, nd, mo, rr, kl, sol_h, res_h, dir_h, leg_h, beam_v, prior_v, ids_s, ids_v, w_h, psi_v,
    noise_s, band_s, table_h, osol_h, ores_h, odir_h,
    sol_v, res_v, dir_v, leg_v, legf, w_v, table_v, yhi, ylo, part, asend, arecv, coef, brecv,
    tiles, basis, prod, sigs, filt, sadj, tt, adj, dsend, drecv, erecv, backf, img, gsend, grecv,
    in_sem, out_sem, b_sem, a_ss, a_rs, c_sem, d_ss, d_rs, e_ss, e_rs, g_ss, g_rs,
):
    n = nb * nd
    days, blk = lax.axis_index("days"), lax.axis_index("blk")
    det, beam = lax.axis_index("det"), lax.axis_index("beam")
    me = blk * nd + det
    kr = rr * kl
    krd = kr // nd
    lt_n = beam_v.shape[1] // LANES
    slots = w_v.shape[0]
    tile_n = P_SIZE // TPIX

    def peer(i):
        t = lax.rem(me + i, n)
        return t, lax.div(t, nd), lax.rem(t, nd)

    loads = [
        pltpu.make_async_copy(src, dst, in_sem.at[i])
        for i, (src, dst) in enumerate(
            [(dir_h, dir_v), (leg_h, leg_v), (table_h, table_v), (w_h, w_v), (res_h, res_v), (sol_h, sol_v)]
        )
    ]
    for copy in loads:
        copy.start()

    barrier = pltpu.get_barrier_semaphore()

    def greet(i):
        _, b, d = peer(i + 1)
        pl.semaphore_signal(barrier, inc=1, device_id=(days, b, d, beam), device_id_type=MESH)

    loop(n - 1, greet)
    for i in range(nd):
        pl.semaphore_signal(
            barrier, inc=1, device_id=(days, blk, lax.rem(det + i, nd), 1 - beam), device_id_type=MESH
        )

    def rows(start, stride):
        return pl.ds(start, mo, stride=stride)

    psi = psi_v[...]
    c1, s1 = jnp.cos(psi), jnp.sin(psi)
    ck, sk = jnp.ones_like(psi), jnp.zeros_like(psi)
    first = beam == 0
    for k in range(kl):
        cn, sn = ck * c1 - sk * s1, sk * c1 + ck * s1
        basis[pl.ds(k, slots, stride=kl), :] = jnp.where(first, ck, sn)
        ck, sk = cn, sn

    loads[0].wait()
    loads[1].wait()
    legf[...] = leg_v[...].astype(F32)
    brecv[beam] = beam_v[...]
    bh = beam_v[...].astype(BF16).astype(F32)
    lhs = jnp.concatenate([bh, beam_v[...] - bh], axis=0).astype(BF16)
    lane = lax.broadcasted_iota(jnp.int32, (kl, LANES), 1)
    keep = lax.rem(lane, HALF) < mo

    def forward(pair):
        for h in range(2):
            r = pair * 2 + h
            for lt in range(lt_n):
                lg = legf[rows(lt * rr + r, lt_n * rr), :]
                for c in range(2):
                    y = dir_v[rows(lt * 2 + c, lt_n * 2), :] * lg
                    yh, yl = split2(y)
                    at = mult(r * LANES + c * HALF, HALF)
                    yhi[pl.ds(at, mo), lt * LANES : (lt + 1) * LANES] = yh
                    ylo[pl.ds(at, mo), lt * LANES : (lt + 1) * LANES] = yl
        span = pl.ds(mult(pair * 2 * LANES, 2 * LANES), 2 * LANES)
        oh = dot_nt(lhs, yhi[span, :])
        ol = dot_nt(lhs, ylo[span, :])
        total = oh[:kl] + (oh[kl:] + ol[:kl])
        for h in range(2):
            at = mult((pair * 2 + h) * kl, kl)
            part[pl.ds(at, kl), :] = jnp.where(keep, total[:, h * LANES : (h + 1) * LANES], 0.0)

    loop(rr // 2, forward)
    asend[...] = part[...].astype(BF16)
    arecv[me] = asend[...]

    pl.semaphore_wait(barrier, n - 1 + nd)

    def a_send(i):
        _, b, d = peer(i + 1)
        pltpu.make_async_remote_copy(
            asend, arecv.at[me], a_ss, a_rs, device_id=(days, b, d, beam), device_id_type=MESH
        ).start()

    loop(n - 1, a_send)
    sister = (days, blk, det, 1 - beam)
    b_copy = pltpu.make_async_remote_copy(
        beam_v, brecv.at[beam], b_sem.at[0], b_sem.at[1], device_id=sister, device_id_type=MESH
    )
    b_copy.start()

    def wait_all(buffer, send_sem, recv_sem):
        some = buffer.at[pl.ds(0, n - 1)]
        pltpu.make_async_copy(some, some, recv_sem).wait()
        pltpu.make_async_copy(some, some, send_sem).wait()

    wait_all(arecv, a_ss, a_rs)

    def add_det(b):
        total = arecv[b * nd].astype(F32)
        for d in range(1, nd):
            total = total + arecv[b * nd + d].astype(F32)
        coef[:, pl.ds(mult(b * LANES, LANES), LANES)] = total.astype(BF16)

    loop(nb, add_det)

    loads[2].wait()
    width = 512
    lhs_c = coef[...]

    def to_pixels(jc):
        out = dot_nn(lhs_c, table_v[:, pl.ds(mult(jc * width, width), width)])
        out = out.astype(BF16).astype(F32)
        for r in range(rr):
            for q in range(width // TPIX):
                tiles[r * tile_n + jc * (width // TPIX) + q] = out[
                    r * kl : (r + 1) * kl, q * TPIX : (q + 1) * TPIX
                ]

    loop(P_SIZE // width, to_pixels)
    loads[3].wait()
    for s in range(slots):
        tile = tiles[ids_s[0, s]].astype(BF16)
        at = slice(s * kl, (s + 1) * kl)
        prod[at, :] = basis[at, :] * dot_nt(tile, w_v[s])
    sig = prod[pl.ds(0, slots, stride=kl), :]
    for k in range(1, kl):
        sig = sig + prod[pl.ds(k, slots, stride=kl), :]
    sigs[beam] = sig
    c_copy = pltpu.make_async_remote_copy(
        sigs.at[beam], sigs.at[beam], c_sem.at[0], c_sem.at[1], device_id=sister, device_id_type=MESH
    )
    c_copy.start()
    c_copy.wait()

    srow = SPD // LANES
    row8 = lax.broadcasted_iota(jnp.int32, (srow, LANES), 0)
    lane8 = lax.broadcasted_iota(jnp.int32, (srow, LANES), 1)
    for d in range(slots // srow):
        at = slice(d * srow, (d + 1) * srow)
        x = sigs[0, at, :] + sigs[1, at, :]
        prev = jnp.where(row8 == 0, 0.0, pltpu.roll(x, 1, 0))
        nxt = jnp.where(row8 == srow - 1, 0.0, pltpu.roll(x, srow - 1, 0))
        center = jnp.float32(0.0)
        total = jnp.zeros_like(x)
        for i in range(1, BW + 1):
            tap = jnp.where(i <= band_s[0, d], noise_s[0, d, i - 1], 0.0)
            center = center + jnp.abs(tap)
            before = jnp.where(lane8 < i, pltpu.roll(prev, i, 1), pltpu.roll(x, i, 1))
            after = jnp.where(
                lane8 >= LANES - i, pltpu.roll(nxt, LANES - i, 1), pltpu.roll(x, LANES - i, 1)
            )
            total = total + tap * (before + after)
        filt[at, :] = (1.0 + 2.0 * center) * x + total

    for s in range(slots):
        at = slice(s * kl, (s + 1) * kl)
        wt = (basis[at, :] * filt[s : s + 1, :]).astype(BF16)
        sadj[at, :] = dot_nn(wt, w_v[s])
    tiles_all = rr * tile_n
    hot = (
        lax.broadcasted_iota(jnp.int32, (tiles_all, slots), 0) == ids_v[...]
    ).astype(F32).astype(BF16)
    xs = jnp.concatenate([sadj[pl.ds(k, slots, stride=kl), :] for k in range(kl)], axis=1)
    xh, xl = split2(xs)
    ts = dot_nn(hot, xh) + dot_nn(hot, xl)
    for k in range(kl):
        tt[pl.ds(k, tiles_all, stride=kl), :] = ts[:, k * TPIX : (k + 1) * TPIX]
    for r in range(rr):
        for q in range(tile_n):
            g = r * tile_n + q
            adj[r * kl : (r + 1) * kl, q * TPIX : (q + 1) * TPIX] = tt[g * kl : (g + 1) * kl, :]
    ah, al = split2(adj[...])
    lhs_a = jnp.concatenate([ah, al], axis=0)

    def to_orders(pair):
        out = dot_nt(lhs_a, table_v[pl.ds(mult(pair * 2 * LANES, 2 * LANES), 2 * LANES), :])
        out = out[:kr] + out[kr:]
        for h in range(2):
            dsend[pair * 2 + h] = out[:, h * LANES : (h + 1) * LANES]

    loop(nb // 2, to_orders)

    def my_rows(d):
        return pl.ds(mult(d * krd, krd), krd)

    def d_send(i):
        _, b, d = peer(i + 1)
        pltpu.make_async_remote_copy(
            dsend.at[b, my_rows(d)], drecv.at[me], d_ss, d_rs,
            device_id=(days, b, d, beam), device_id_type=MESH,
        ).start()

    loop(n - 1, d_send)
    drecv[me] = dsend[blk, my_rows(det), :]
    wait_all(drecv, d_ss, d_rs)
    back = drecv[0]
    for i in range(1, n):
        back = back + drecv[i]
    erecv[beam, det] = back.astype(BF16)
    e_copies = []
    for bm in range(2):
        for i in range(nd):
            if bm == 0 and i == 0:
                continue
            mine = erecv.at[beam, det]
            e_copies.append(
                pltpu.make_async_remote_copy(
                    mine, mine, e_ss.at[len(e_copies)], e_rs.at[len(e_copies)],
                    device_id=(days, blk, lax.rem(det + i, nd), beam if bm == 0 else 1 - beam),
                    device_id_type=MESH,
                )
            )
    for copy in e_copies:
        copy.start()
    loads[4].wait()
    loads[5].wait()
    b_copy.wait()
    bm_all = jnp.concatenate([brecv[0], brecv[1]], axis=0)
    gh = bm_all.astype(BF16)
    rhs_b = jnp.concatenate([gh, (bm_all - gh.astype(F32)).astype(BF16)], axis=0)
    for copy in e_copies:
        copy.wait()
    for bm in range(2):
        for d in range(nd):
            backf[bm, d * krd : (d + 1) * krd, :] = erecv[bm, d].astype(F32)

    for lt in range(lt_n):
        for c in range(2):
            at = lt * 2 + c
            img[rows(at, lt_n * 2), :] = prior_v[lt : lt + 1, :] * dir_v[rows(at, lt_n * 2), :]

    def to_image(r):
        at = pl.ds(mult(r * kl, kl), kl)
        b0, b1 = backf[0, at, :], backf[1, at, :]
        lb = jnp.concatenate([b0, b1, b0, b1], axis=0).astype(BF16)
        g = dot_tn(lb, rhs_b)
        for lt in range(lt_n):
            lg = legf[rows(lt * rr + r, lt_n * rr), :]
            for c in range(2):
                to = rows(lt * 2 + c, lt_n * 2)
                img[to, :] = img[to, :] + lg * g[
                    c * HALF : c * HALF + mo, lt * LANES : (lt + 1) * LANES
                ]

    loop(rr, to_image)

    acc = None
    for q in range(lt_n * 2):
        at = rows(q, lt_n * 2)
        rv, dv, iv = res_v[at, :], dir_v[at, :], img[at, :]
        terms = [rv * rv, dv * iv, rv * iv, iv * iv]
        acc = terms if acc is None else [a + t for a, t in zip(acc, terms)]
    gsend[...] = jnp.zeros_like(gsend)
    for i, a in enumerate(acc):
        gsend[i : i + 1, :] = jnp.sum(a, axis=0, keepdims=True)

    def g_send(i):
        _, b, d = peer(i + 1)
        pltpu.make_async_remote_copy(
            gsend, grecv.at[me], g_ss, g_rs, device_id=(days, b, d, beam), device_id_type=MESH
        ).start()

    loop(n - 1, g_send)
    grecv[me] = gsend[...]
    wait_all(grecv, g_ss, g_rs)
    tot = grecv[0]
    for i in range(1, n):
        tot = tot + grecv[i]
    sums = jnp.sum(tot, axis=1, keepdims=True)
    rr_sum, di_sum, ri_sum, ii_sum = (sums[i : i + 1, :] for i in range(4))
    alpha = rr_sum / di_sum
    new_norm = rr_sum - 2.0 * alpha * ri_sum + alpha * alpha * ii_sum
    beta = new_norm / rr_sum
    dv = dir_v[...]
    nr = res_v[...] - alpha * img[...]
    res_v[...] = nr
    o_res = pltpu.make_async_copy(res_v, ores_h, out_sem.at[0])
    o_res.start()
    sol_v[...] = sol_v[...] + alpha * dv
    o_sol = pltpu.make_async_copy(sol_v, osol_h, out_sem.at[1])
    o_sol.start()
    img[...] = nr + beta * dv
    o_dir = pltpu.make_async_copy(img, odir_h, out_sem.at[2])
    o_dir.start()
    o_res.wait()
    o_sol.wait()
    o_dir.wait()


def flat(x):
    a, m, l = x.shape
    y = jnp.transpose(x, (1, 0, 2)).reshape(m, a, l // LANES, LANES)
    return jnp.transpose(y, (0, 2, 1, 3)).reshape(m * l // LANES * a, LANES)


def unflat(y, a, m, l):
    x = jnp.transpose(y.reshape(m, l // LANES, a, LANES), (0, 2, 1, 3)).reshape(m, a, l)
    return jnp.transpose(x, (1, 0, 2))


def body(
    nb, nd, table, solution, residual, direction, legendre, beam_coef, prior_weight, tile_ids,
    interp_weight, psi_angle, noise_coef, band_width,
):
    _, mo, ll = direction.shape
    rr = legendre.shape[2]
    kl = beam_coef.shape[1]
    slots = tile_ids.shape[1]
    n = nb * nd
    kr = rr * kl
    frows = 2 * mo * ll // LANES
    lrows = rr * mo * ll // LANES
    tiles_all = rr * (P_SIZE // TPIX)
    any_spec = pl.BlockSpec(memory_space=pl.ANY)
    vmem = pl.BlockSpec(memory_space=pltpu.VMEM)
    smem = pl.BlockSpec(memory_space=pltpu.SMEM)
    V = pltpu.VMEM
    dma = pltpu.SemaphoreType.DMA
    flat_shape = jax.ShapeDtypeStruct((frows, LANES), F32)
    outs = pl.pallas_call(
        functools.partial(kernel, nb, nd, mo, rr, kl),
        out_shape=(flat_shape,) * 3,
        in_specs=[any_spec] * 4 + [vmem, vmem, smem, vmem, any_spec, vmem, smem, smem, any_spec],
        out_specs=(any_spec,) * 3,
        scratch_shapes=[
            V((frows, LANES), F32), V((frows, LANES), F32), V((frows, LANES), F32),
            V((lrows, LANES), BF16), V((lrows, LANES), F32),
            V((slots, LANES, TPIX), BF16), V((nb * LANES, P_SIZE), BF16),
            V((rr * LANES, ll), BF16), V((rr * LANES, ll), BF16),
            V((kr, LANES), F32), V((kr, LANES), BF16), V((n, kr, LANES), BF16),
            V((kr, nb * LANES), BF16), V((2, kl, ll), F32),
            V((tiles_all, kl, TPIX), F32), V((slots * kl, LANES), F32), V((slots * kl, LANES), F32),
            V((2, slots, LANES), F32), V((slots, LANES), F32), V((slots * kl, TPIX), F32),
            V((tiles_all * kl, TPIX), F32), V((kr, P_SIZE), F32),
            V((nb, kr, LANES), F32), V((n, kr // nd, LANES), F32),
            V((2, nd, kr // nd, LANES), BF16), V((2, kr, LANES), F32),
            V((frows, LANES), F32), V((8, LANES), F32), V((n, 8, LANES), F32),
            dma((6,)), dma((3,)), dma((2,)), dma, dma, dma((2,)), dma, dma,
            dma((2 * nd - 1,)), dma((2 * nd - 1,)), dma, dma,
        ],
        compiler_params=pltpu.CompilerParams(
            collective_id=0, has_side_effects=True, vmem_limit_bytes=60 * 1024 * 1024
        ),
        name="cg_step",
    )(
        flat(solution), flat(residual), flat(direction), flat(jnp.transpose(legendre, (2, 0, 1))),
        jnp.transpose(beam_coef), prior_weight.reshape(ll // LANES, LANES), tile_ids, tile_ids,
        interp_weight[0], psi_angle[0], noise_coef, band_width, table,
    )
    return tuple(unflat(o, 2, mo, ll) for o in outs)


def solution(mesh):
    nb, nd = mesh.shape["blk"], mesh.shape["det"]
    field = P(None, ("days", "blk"), "det")
    spans = ("days", "blk", "det")
    in_specs = (
        field, field, field, P("blk", "det", None), P("det", "beam"), P("det"), P(spans, None),
        P(spans, None, None, None), P(spans, None, None), P(spans, None, None), P(spans, None),
    )

    def run(*args):
        orders = args[2].shape[1] // (nb * mesh.shape["days"])
        table = padded_table(nb, orders)
        return jax.shard_map(
            functools.partial(body, nb, nd, jnp.asarray(table)),
            mesh=mesh, in_specs=in_specs, out_specs=(field,) * 3, check_vma=False,
        )(*args)

    return run
```

time: 164 us -> 33.4 us (0.20)
  blocking collectives: 79.4 us -> 0 us
  Pallas kernels: 0 us -> 27.4 us
  waiting for transfers between devices: 23 us -> 0 us
  between operations: 17 us -> 0.64 us
  starting transfers between devices: 15.9 us -> 0 us
  other arithmetic: 11.5 us -> 0 us
  matrix products: 9 us -> 0 us
  local copies, waits for them, and re-layouts: 7.95 us -> 5.02 us
    psum x5 -> x0, blocking collectives: 57.2 us -> none  [the longest x1 22.3 us: body(): old_norm = lax.psum(jnp.sum(residual * residual), ('blk', 'det'))]
    pallas_call x0 -> x1, Pallas kernels: none -> 27.4 us  [body(): pl.pallas_call(functools.partial(kernel, nb, nd, mo, rr, kl), out_shape=(...]
    all_to_all x3 -> x0, starting transfers between devices: 15.9 us -> none  [the longest x1 6.32 us: body(): lax.all_to_all(partial_value, 'blk', split_axis=3, concat_axis=2, tiled=T...]
    psum x1 -> x0, waiting for transfers between devices: 14.9 us -> none  [body(): lax.psum(image_part, 'beam') + prior_weight[None, None, :] * direction]
    all_gather x1 -> x0, blocking collectives: 14 us -> none  [body(): every_tile = lax.all_gather(cycle_tiles, 'blk', axis=1, tiled=True)]
    dot_general x13 -> x0, matrix products: 9 us -> none  [the longest x1 3.61 us: body(): jnp.einsum('ckml,mlr->ckmr', scaled, legendre, preferred_element_type=jnp...]
    all_to_all x1 -> x0, blocking collectives: 8.15 us -> none  [body(): lax.all_to_all(back_coef, 'blk', split_axis=2, concat_axis=3, tiled=True)]
    all_to_all x3 -> x0, waiting for transfers between devices: 8.12 us -> none  [the longest x1 8.12 us: body(): lax.all_to_all(outgoing, 'blk', split_axis=0, concat_axis=0, tiled=True)]
  transfers between devices with their start and end apart: 4 -> 0, of which waited for: 2 -> 0; matrix products, arithmetic and copies ran while one was open for 9% -> 0% of each run, Pallas kernels for 0% -> 0%
where the time goes in v1:
time: 33.4 us; the launch traced here: 33.1 us
  Pallas kernels  27.4 us (82%)
  local copies, waits for them, and re-layouts  5.02 us (15%)
  between operations  0.64 us (2%)
    pallas_call x1, Pallas kernels, body(): pl.pallas_call(functools.partial(kernel, nb, nd, mo, rr, kl), out_shape=(...  27.4 us
    unnamed x3, local copies, waits for them, and re-layouts  5.02 us

profile of v1, /device:TPU:0, one launch (start us, length us, event | category | flops | bytes accessed | tf_op | source)
XLA Modules:
  0.0 33.1 jit_solution(3250531091355686538)
XLA Ops:
  0.6 27.4 %cg_step.1 = (f32[528,128]{1,0:T(8,128)}, f32[528,128]{1,0:T(8,128)}, f32[528,128]{1,0:T(8,128)}) custom-call(f32[528,128]{1,0:T(8,128)} %bitcast.57, f32[528,128]{1,0:T(8,128)} %bitcast.58, f32[528,128]{1,0:T(8,128)} %bitcast.59, bf16[1056,128]{1,0:T(8,128)(2,1)} %bitcast.60, f32[8,1024]{1,0:T(8,128)} %bitcast.61, f32[8,128]{1,0:T(8,128)} %bitcast.63, ...), custom_call_target="tpu_custom_call" | custom-call | tf_op jit(solution)/shard_map/cg_step/pallas_call | solution.py:398
  28.1 1.7 %copy.22 = f32[2,33,1024]{2,0,1:T(2,128)} copy(f32[2,33,1024]{2,0,1:T(2,128)} %bitcast.56) | data formatting | bytes 540672
  29.7 1.7 %copy.23 = f32[2,33,1024]{2,0,1:T(2,128)} copy(f32[2,33,1024]{2,0,1:T(2,128)} %bitcast.55) | data formatting | bytes 540672
  31.4 1.7 %copy.24 = f32[2,33,1024]{2,0,1:T(2,128)} copy(f32[2,33,1024]{2,0,1:T(2,128)} %bitcast.54) | data formatting | bytes 540672

commit v2 on v1

--- a/solution.py
+++ b/solution.py
@@ -66,18 +66,18 @@
 
 
 def kernel(
-    nb, nd, mo, rr, kl, sol_h, res_h, dir_h, leg_h, beam_v, prior_v, ids_s, ids_v, w_h, psi_v,
-    noise_s, band_s, table_h, osol_h, ores_h, odir_h,
-    sol_v, res_v, dir_v, leg_v, legf, w_v, table_v, yhi, ylo, part, asend, arecv, coef, brecv,
-    tiles, basis, prod, sigs, filt, sadj, tt, adj, dsend, drecv, erecv, backf, img, gsend, grecv,
-    in_sem, out_sem, b_sem, a_ss, a_rs, c_sem, d_ss, d_rs, e_ss, e_rs, g_ss, g_rs,
+    nb, nd, mo, rr, kl, two, res_h, dir_h, leg_h, beam_v, prior_v, ids_s, ids_v, w_h, psi_v,
+    noise_s, band_s, table_h, back_h, img, sums_v,
+    res_v, dir_v, leg_v, legf, w_v, table_v, back_s, yhi, ylo, part, asend, arecv, coef, brecv,
+    tiles, basis, prod, sigs, filt, sadj, tt, adj, dsend, drecv, erecv, backf, gsend, grecv,
+    in_sem, b_sem, a_ss, a_rs, c_sem, d_ss, d_rs, e_ss, e_rs, g_ss, g_rs,
 ):
     n = nb * nd
+    back_v = back_s if two else None
     days, blk = lax.axis_index("days"), lax.axis_index("blk")
     det, beam = lax.axis_index("det"), lax.axis_index("beam")
     me = blk * nd + det
     kr = rr * kl
-    krd = kr // nd
     lt_n = beam_v.shape[1] // LANES
     slots = w_v.shape[0]
     tile_n = P_SIZE // TPIX
@@ -89,9 +89,11 @@
     loads = [
         pltpu.make_async_copy(src, dst, in_sem.at[i])
         for i, (src, dst) in enumerate(
-            [(dir_h, dir_v), (leg_h, leg_v), (table_h, table_v), (w_h, w_v), (res_h, res_v), (sol_h, sol_v)]
+            [(dir_h, dir_v), (leg_h, leg_v), (table_h, table_v), (w_h, w_v), (res_h, res_v)]
         )
     ]
+    if two:
+        loads.append(pltpu.make_async_copy(back_h, back_s, in_sem.at[5]))
     for copy in loads:
         copy.start()
 
@@ -102,22 +104,10 @@
         pl.semaphore_signal(barrier, inc=1, device_id=(days, b, d, beam), device_id_type=MESH)
 
     loop(n - 1, greet)
-    for i in range(nd):
-        pl.semaphore_signal(
-            barrier, inc=1, device_id=(days, blk, lax.rem(det + i, nd), 1 - beam), device_id_type=MESH
-        )
+    pl.semaphore_signal(barrier, inc=1, device_id=(days, blk, det, 1 - beam), device_id_type=MESH)
 
     def rows(start, stride):
         return pl.ds(start, mo, stride=stride)
-
-    psi = psi_v[...]
-    c1, s1 = jnp.cos(psi), jnp.sin(psi)
-    ck, sk = jnp.ones_like(psi), jnp.zeros_like(psi)
-    first = beam == 0
-    for k in range(kl):
-        cn, sn = ck * c1 - sk * s1, sk * c1 + ck * s1
-        basis[pl.ds(k, slots, stride=kl), :] = jnp.where(first, ck, sn)
-        ck, sk = cn, sn
 
     loads[0].wait()
     loads[1].wait()
@@ -140,8 +130,8 @@
                     yhi[pl.ds(at, mo), lt * LANES : (lt + 1) * LANES] = yh
                     ylo[pl.ds(at, mo), lt * LANES : (lt + 1) * LANES] = yl
         span = pl.ds(mult(pair * 2 * LANES, 2 * LANES), 2 * LANES)
-        oh = dot_nt(lhs, yhi[span, :])
-        ol = dot_nt(lhs, ylo[span, :])
+        oh = dot_nt(yhi[span, :], lhs).T
+        ol = dot_nt(ylo[span, :], lhs).T
         total = oh[:kl] + (oh[kl:] + ol[:kl])
         for h in range(2):
             at = mult((pair * 2 + h) * kl, kl)
@@ -151,7 +141,7 @@
     asend[...] = part[...].astype(BF16)
     arecv[me] = asend[...]
 
-    pl.semaphore_wait(barrier, n - 1 + nd)
+    pl.semaphore_wait(barrier, n)
 
     def a_send(i):
         _, b, d = peer(i + 1)
@@ -170,6 +160,15 @@
         some = buffer.at[pl.ds(0, n - 1)]
         pltpu.make_async_copy(some, some, recv_sem).wait()
         pltpu.make_async_copy(some, some, send_sem).wait()
+
+    psi = psi_v[...]
+    c1, s1 = jnp.cos(psi), jnp.sin(psi)
+    ck, sk = jnp.ones_like(psi), jnp.zeros_like(psi)
+    first = beam == 0
+    for k in range(kl):
+        cn, sn = ck * c1 - sk * s1, sk * c1 + ck * s1
+        basis[pl.ds(k, slots, stride=kl), :] = jnp.where(first, ck, sn)
+        ck, sk = cn, sn
 
     wait_all(arecv, a_ss, a_rs)
 
@@ -247,51 +246,45 @@
         for q in range(tile_n):
             g = r * tile_n + q
             adj[r * kl : (r + 1) * kl, q * TPIX : (q + 1) * TPIX] = tt[g * kl : (g + 1) * kl, :]
+    if two:
+        loads[5].wait()
     ah, al = split2(adj[...])
     lhs_a = jnp.concatenate([ah, al], axis=0)
 
     def to_orders(pair):
-        out = dot_nt(lhs_a, table_v[pl.ds(mult(pair * 2 * LANES, 2 * LANES), 2 * LANES), :])
+        span = pl.ds(mult(pair * 2 * LANES, 2 * LANES), 2 * LANES)
+        if back_v is None:
+            out = dot_nt(lhs_a, table_v[span, :])
+        else:
+            out = dot_nn(lhs_a, back_v[:, span])
         out = out[:kr] + out[kr:]
         for h in range(2):
-            dsend[pair * 2 + h] = out[:, h * LANES : (h + 1) * LANES]
+            dsend[pair * 2 + h] = out[:, h * LANES : (h + 1) * LANES].astype(BF16)
 
     loop(nb // 2, to_orders)
-
-    def my_rows(d):
-        return pl.ds(mult(d * krd, krd), krd)
 
     def d_send(i):
         _, b, d = peer(i + 1)
         pltpu.make_async_remote_copy(
-            dsend.at[b, my_rows(d)], drecv.at[me], d_ss, d_rs,
+            dsend.at[b], drecv.at[me], d_ss, d_rs,
             device_id=(days, b, d, beam), device_id_type=MESH,
         ).start()
 
     loop(n - 1, d_send)
-    drecv[me] = dsend[blk, my_rows(det), :]
+    drecv[me] = dsend[blk]
     wait_all(drecv, d_ss, d_rs)
-    back = drecv[0]
+    back = drecv[0].astype(F32)
     for i in range(1, n):
-        back = back + drecv[i]
-    erecv[beam, det] = back.astype(BF16)
-    e_copies = []
-    for bm in range(2):
-        for i in range(nd):
-            if bm == 0 and i == 0:
-                continue
-            mine = erecv.at[beam, det]
-            e_copies.append(
-                pltpu.make_async_remote_copy(
-                    mine, mine, e_ss.at[len(e_copies)], e_rs.at[len(e_copies)],
-                    device_id=(days, blk, lax.rem(det + i, nd), beam if bm == 0 else 1 - beam),
-                    device_id_type=MESH,
-                )
-            )
+        back = back + drecv[i].astype(F32)
+    erecv[beam] = back.astype(BF16)
+    e_copies = [
+        pltpu.make_async_remote_copy(
+            erecv.at[beam], erecv.at[beam], e_ss, e_rs, device_id=sister, device_id_type=MESH
+        )
+    ]
     for copy in e_copies:
         copy.start()
     loads[4].wait()
-    loads[5].wait()
     b_copy.wait()
     bm_all = jnp.concatenate([brecv[0], brecv[1]], axis=0)
     gh = bm_all.astype(BF16)
@@ -299,8 +292,7 @@
     for copy in e_copies:
         copy.wait()
     for bm in range(2):
-        for d in range(nd):
-            backf[bm, d * krd : (d + 1) * krd, :] = erecv[bm, d].astype(F32)
+        backf[bm] = erecv[bm].astype(F32)
 
     for lt in range(lt_n):
         for c in range(2):
@@ -344,25 +336,20 @@
     tot = grecv[0]
     for i in range(1, n):
         tot = tot + grecv[i]
-    sums = jnp.sum(tot, axis=1, keepdims=True)
+    sums_v[...] = tot
+
+
+def update_kernel(sol_v, res_v, dir_v, img_v, sums_v, osol_v, ores_v, odir_v):
+    sums = jnp.sum(sums_v[...], axis=1, keepdims=True)
     rr_sum, di_sum, ri_sum, ii_sum = (sums[i : i + 1, :] for i in range(4))
     alpha = rr_sum / di_sum
     new_norm = rr_sum - 2.0 * alpha * ri_sum + alpha * alpha * ii_sum
     beta = new_norm / rr_sum
     dv = dir_v[...]
-    nr = res_v[...] - alpha * img[...]
-    res_v[...] = nr
-    o_res = pltpu.make_async_copy(res_v, ores_h, out_sem.at[0])
-    o_res.start()
-    sol_v[...] = sol_v[...] + alpha * dv
-    o_sol = pltpu.make_async_copy(sol_v, osol_h, out_sem.at[1])
-    o_sol.start()
-    img[...] = nr + beta * dv
-    o_dir = pltpu.make_async_copy(img, odir_h, out_sem.at[2])
-    o_dir.start()
-    o_res.wait()
-    o_sol.wait()
-    o_dir.wait()
+    nr = res_v[...] - alpha * img_v[...]
+    ores_v[...] = nr
+    osol_v[...] = sol_v[...] + alpha * dv
+    odir_v[...] = nr + beta * dv
 
 
 def flat(x):
@@ -377,10 +364,12 @@
 
 
 def body(
-    nb, nd, table, solution, residual, direction, legendre, beam_coef, prior_weight, tile_ids,
+    nb, nd, table_np, solution, residual, direction, legendre, beam_coef, prior_weight, tile_ids,
     interp_weight, psi_angle, noise_coef, band_width,
 ):
     _, mo, ll = direction.shape
+    table = jnp.asarray(table_np)
+    two = nb <= 8
     rr = legendre.shape[2]
     kl = beam_coef.shape[1]
     slots = tile_ids.shape[1]
@@ -395,36 +384,46 @@
     V = pltpu.VMEM
     dma = pltpu.SemaphoreType.DMA
     flat_shape = jax.ShapeDtypeStruct((frows, LANES), F32)
-    outs = pl.pallas_call(
-        functools.partial(kernel, nb, nd, mo, rr, kl),
-        out_shape=(flat_shape,) * 3,
-        in_specs=[any_spec] * 4 + [vmem, vmem, smem, vmem, any_spec, vmem, smem, smem, any_spec],
-        out_specs=(any_spec,) * 3,
-        scratch_shapes=[
-            V((frows, LANES), F32), V((frows, LANES), F32), V((frows, LANES), F32),
-            V((lrows, LANES), BF16), V((lrows, LANES), F32),
-            V((slots, LANES, TPIX), BF16), V((nb * LANES, P_SIZE), BF16),
-            V((rr * LANES, ll), BF16), V((rr * LANES, ll), BF16),
-            V((kr, LANES), F32), V((kr, LANES), BF16), V((n, kr, LANES), BF16),
-            V((kr, nb * LANES), BF16), V((2, kl, ll), F32),
-            V((tiles_all, kl, TPIX), F32), V((slots * kl, LANES), F32), V((slots * kl, LANES), F32),
-            V((2, slots, LANES), F32), V((slots, LANES), F32), V((slots * kl, TPIX), F32),
-            V((tiles_all * kl, TPIX), F32), V((kr, P_SIZE), F32),
-            V((nb, kr, LANES), F32), V((n, kr // nd, LANES), F32),
-            V((2, nd, kr // nd, LANES), BF16), V((2, kr, LANES), F32),
-            V((frows, LANES), F32), V((8, LANES), F32), V((n, 8, LANES), F32),
-            dma((6,)), dma((3,)), dma((2,)), dma, dma, dma((2,)), dma, dma,
-            dma((2 * nd - 1,)), dma((2 * nd - 1,)), dma, dma,
-        ],
+    sol, res, dirn = flat(solution), flat(residual), flat(direction)
+    scratch = [
+        V((frows, LANES), F32), V((frows, LANES), F32),
+        V((lrows, LANES), BF16), V((lrows, LANES), F32),
+        V((slots, LANES, TPIX), BF16), V((nb * LANES, P_SIZE), BF16),
+        V((P_SIZE, nb * LANES) if two else (16, LANES), BF16),
+        V((rr * LANES, ll), BF16), V((rr * LANES, ll), BF16),
+        V((kr, LANES), F32), V((kr, LANES), BF16), V((n, kr, LANES), BF16),
+        V((kr, nb * LANES), BF16), V((2, kl, ll), F32),
+        V((tiles_all, kl, TPIX), F32), V((slots * kl, LANES), F32), V((slots * kl, LANES), F32),
+        V((2, slots, LANES), F32), V((slots, LANES), F32), V((slots * kl, TPIX), F32),
+        V((tiles_all * kl, TPIX), F32), V((kr, P_SIZE), F32),
+        V((nb, kr, LANES), BF16), V((n, kr, LANES), BF16),
+        V((2, kr, LANES), BF16), V((2, kr, LANES), F32),
+        V((8, LANES), F32), V((n, 8, LANES), F32),
+        dma((6,)), dma((2,)), dma, dma, dma((2,)), dma, dma,
+        dma, dma, dma, dma,
+    ]
+    held = sum(
+        math.prod(v.shape) * v.dtype.itemsize for v in scratch if hasattr(v, 'dtype') and getattr(v, 'memory_space', None) == V)
+    grant = held + held // 8 + 6 * 1024 * 1024
+    image, sums = pl.pallas_call(
+        functools.partial(kernel, nb, nd, mo, rr, kl, two),
+        out_shape=(flat_shape, jax.ShapeDtypeStruct((8, LANES), F32)),
+        in_specs=[any_spec] * 3 + [vmem, vmem, smem, vmem, any_spec, vmem, smem, smem, any_spec, any_spec],
+        out_specs=(vmem, vmem),
+        scratch_shapes=scratch,
         compiler_params=pltpu.CompilerParams(
             collective_id=0, has_side_effects=True, vmem_limit_bytes=60 * 1024 * 1024
         ),
         name="cg_step",
     )(
-        flat(solution), flat(residual), flat(direction), flat(jnp.transpose(legendre, (2, 0, 1))),
+        res, dirn, flat(jnp.transpose(legendre, (2, 0, 1))),
         jnp.transpose(beam_coef), prior_weight.reshape(ll // LANES, LANES), tile_ids, tile_ids,
-        interp_weight[0], psi_angle[0], noise_coef, band_width, table,
+        interp_weight[0], psi_angle[0], noise_coef, band_width, table, jnp.asarray(table_np.T) if two else table[:16],
     )
+    outs = pl.pallas_call(
+        update_kernel, out_shape=(flat_shape,) * 3, in_specs=[vmem] * 5, out_specs=(vmem,) * 3,
+        name="cg_update",
+    )(sol, res, dirn, image, sums)
     return tuple(unflat(o, 2, mo, ll) for o in outs)
 
 
@@ -441,7 +440,7 @@
         orders = args[2].shape[1] // (nb * mesh.shape["days"])
         table = padded_table(nb, orders)
         return jax.shard_map(
-            functools.partial(body, nb, nd, jnp.asarray(table)),
+            functools.partial(body, nb, nd, table),
             mesh=mesh, in_specs=in_specs, out_specs=(field,) * 3, check_vma=False,
         )(*args)
 

time: 33.4 us -> 28.8 us (0.86)
  local copies, waits for them, and re-layouts: 5.02 us -> 0 us
  Pallas kernels: 27.4 us -> 27.9 us
    unnamed x3 -> x0, local copies, waits for them, and re-layouts: 5.02 us -> none
    pallas_call x1 -> x2, Pallas kernels: 27.4 us -> 27.9 us  [the longest x1 25.6 us: body(): pl.pallas_call(functools.partial(kernel, nb, nd, mo, rr, kl, two), out_sh...]
where the time goes in v2:
time: 28.8 us; the launch traced here: 28.5 us
  Pallas kernels  27.9 us (97%)
  between operations  0.64 us (2%)
    pallas_call x1, Pallas kernels, body(): pl.pallas_call(functools.partial(kernel, nb, nd, mo, rr, kl, two), out_sh...  25.6 us
    pallas_call x1, Pallas kernels, body(): pl.pallas_call(update_kernel, out_shape=(flat_shape,) * 3, in_specs=[vmem...  2.26 us

profile of v2, /device:TPU:0, one launch (start us, length us, event | category | flops | bytes accessed | tf_op | source)
XLA Modules:
  0.0 28.5 jit_solution(5245714529703863560)
XLA Ops:
  0.6 25.6 %cg_step.1 = (f32[528,128]{1,0:T(8,128)}, f32[8,128]{1,0:T(8,128)}) custom-call(f32[528,128]{1,0:T(8,128)} %bitcast.53, f32[528,128]{1,0:T(8,128)} %bitcast.55, bf16[1056,128]{1,0:T(8,128)(2,1)} %bitcast.58, f32[8,1024]{1,0:T(8,128)} %bitcast.60, f32[8,128]{1,0:T(8,128)} %bitcast.62, s32[1,32]{1,0:T(1,128)} %ids_v.1, s32[1,32]{1,0:T(1,128)} %ids_v.1, ...), custom_call_target="tpu_custom_call" | custom-call | tf_op jit(solution)/shard_map/cg_step/pallas_call | solution.py:408
  26.3 2.3 %cg_update.1 = (f32[528,128]{1,0:T(8,128)}, f32[528,128]{1,0:T(8,128)}, f32[528,128]{1,0:T(8,128)}) custom-call(f32[528,128]{1,0:T(8,128)} %bitcast.59, f32[528,128]{1,0:T(8,128)} %bitcast.54, f32[528,128]{1,0:T(8,128)} %bitcast.56, f32[528,128]{1,0:T(8,128)} %get-tuple-element.8.img_v, f32[8,128]{1,0:T(8,128)} %get-tuple-element.9.sums_v), custom_call_target="tpu_custom_call" | custom-call | tf_op jit(solution)/shard_map/cg_update/pallas_call | solution.py:423

commit v3 on v2

--- a/solution.py
+++ b/solution.py
@@ -16,7 +16,7 @@
 SPD = 1024
 BW = 8
 LANES = 128
-HALF = 64
+HALF = 48
 F32 = jnp.float32
 BF16 = jnp.bfloat16
 MESH = pl.DeviceIdType.MESH
@@ -30,9 +30,9 @@
         2.0 * math.pi / P_SIZE
     )
     scale = np.float32(1.0 / math.sqrt(2.0 * total))
-    table = np.zeros((blocks, 2, HALF, P_SIZE), np.float32)
-    table[:, 0, :orders] = (np.cos(phase) * scale).reshape(blocks, orders, P_SIZE)
-    table[:, 1, :orders] = (-np.sin(phase) * scale).reshape(blocks, orders, P_SIZE)
+    table = np.zeros((blocks, LANES, P_SIZE), np.float32)
+    table[:, :orders] = (np.cos(phase) * scale).reshape(blocks, orders, P_SIZE)
+    table[:, HALF : HALF + orders] = (-np.sin(phase) * scale).reshape(blocks, orders, P_SIZE)
     return table.reshape(blocks * LANES, P_SIZE).astype(ml_dtypes.bfloat16)
 
 
@@ -83,7 +83,12 @@
     tile_n = P_SIZE // TPIX
 
     def peer(i):
-        t = lax.rem(me + i, n)
+        if isinstance(i, int) and n & (n - 1) == 0:
+            t = me
+            for bit in [1 << q for q in range(n.bit_length() - 1) if (n - i) >> q & 1]:
+                t = t + bit * (1 - 2 * lax.rem(lax.div(me, bit), 2))
+        else:
+            t = lax.rem(me + i, n)
         return t, lax.div(t, nd), lax.rem(t, nd)
 
     loads = [
@@ -116,7 +121,7 @@
     bh = beam_v[...].astype(BF16).astype(F32)
     lhs = jnp.concatenate([bh, beam_v[...] - bh], axis=0).astype(BF16)
     lane = lax.broadcasted_iota(jnp.int32, (kl, LANES), 1)
-    keep = lax.rem(lane, HALF) < mo
+    keep = (lax.rem(lane, HALF) < mo) & (lane < 2 * HALF)
 
     def forward(pair):
         for h in range(2):
@@ -126,7 +131,7 @@
                 for c in range(2):
                     y = dir_v[rows(lt * 2 + c, lt_n * 2), :] * lg
                     yh, yl = split2(y)
-                    at = mult(r * LANES + c * HALF, HALF)
+                    at = mult(r * LANES + c * HALF, 16)
                     yhi[pl.ds(at, mo), lt * LANES : (lt + 1) * LANES] = yh
                     ylo[pl.ds(at, mo), lt * LANES : (lt + 1) * LANES] = yl
         span = pl.ds(mult(pair * 2 * LANES, 2 * LANES), 2 * LANES)
@@ -156,10 +161,12 @@
     )
     b_copy.start()
 
+    sent = []
+
     def wait_all(buffer, send_sem, recv_sem):
         some = buffer.at[pl.ds(0, n - 1)]
         pltpu.make_async_copy(some, some, recv_sem).wait()
-        pltpu.make_async_copy(some, some, send_sem).wait()
+        sent.append((some, send_sem))
 
     psi = psi_v[...]
     c1, s1 = jnp.cos(psi), jnp.sin(psi)
@@ -294,32 +301,47 @@
     for bm in range(2):
         backf[bm] = erecv[bm].astype(F32)
 
-    for lt in range(lt_n):
-        for c in range(2):
-            at = lt * 2 + c
-            img[rows(at, lt_n * 2), :] = prior_v[lt : lt + 1, :] * dir_v[rows(at, lt_n * 2), :]
-
-    def to_image(r):
+    def spread(r):
         at = pl.ds(mult(r * kl, kl), kl)
         b0, b1 = backf[0, at, :], backf[1, at, :]
-        lb = jnp.concatenate([b0, b1, b0, b1], axis=0).astype(BF16)
-        g = dot_tn(lb, rhs_b)
-        for lt in range(lt_n):
-            lg = legf[rows(lt * rr + r, lt_n * rr), :]
-            for c in range(2):
-                to = rows(lt * 2 + c, lt_n * 2)
-                img[to, :] = img[to, :] + lg * g[
-                    c * HALF : c * HALF + mo, lt * LANES : (lt + 1) * LANES
-                ]
-
-    loop(rr, to_image)
+        lb = jnp.concatenate([b0, b1, b0, b1], axis=0)[:, : 2 * HALF].astype(BF16)
+        return dot_tn(lb, rhs_b)
 
     acc = None
-    for q in range(lt_n * 2):
-        at = rows(q, lt_n * 2)
-        rv, dv, iv = res_v[at, :], dir_v[at, :], img[at, :]
-        terms = [rv * rv, dv * iv, rv * iv, iv * iv]
-        acc = terms if acc is None else [a + t for a, t in zip(acc, terms)]
+    if rr <= 4:
+        fields = [spread(r) for r in range(rr)]
+    else:
+        for q in range(lt_n * 2):
+            at = rows(q, lt_n * 2)
+            img[at, :] = jnp.zeros((mo, LANES), F32)
+
+        def to_image(r):
+            g = spread(r)
+            for lt in range(lt_n):
+                lg = legf[rows(lt * rr + r, lt_n * rr), :]
+                for c in range(2):
+                    to = rows(lt * 2 + c, lt_n * 2)
+                    img[to, :] = img[to, :] + lg * g[
+                        c * HALF : c * HALF + mo, lt * LANES : (lt + 1) * LANES
+                    ]
+
+        loop(rr, to_image)
+
+    for lt in range(lt_n):
+        if rr <= 4:
+            lgs = [legf[rows(lt * rr + r, lt_n * rr), :] for r in range(rr)]
+        for c in range(2):
+            at = rows(lt * 2 + c, lt_n * 2)
+            dv, rv = dir_v[at, :], res_v[at, :]
+            iv = prior_v[lt : lt + 1, :] * dv
+            if rr <= 4:
+                for lg, g in zip(lgs, fields):
+                    iv = iv + lg * g[c * HALF : c * HALF + mo, lt * LANES : (lt + 1) * LANES]
+            else:
+                iv = iv + img[at, :]
+            img[at, :] = iv
+            terms = [rv * rv, dv * iv, rv * iv, iv * iv]
+            acc = terms if acc is None else [a + t for a, t in zip(acc, terms)]
     gsend[...] = jnp.zeros_like(gsend)
     for i, a in enumerate(acc):
         gsend[i : i + 1, :] = jnp.sum(a, axis=0, keepdims=True)
@@ -337,6 +359,8 @@
     for i in range(1, n):
         tot = tot + grecv[i]
     sums_v[...] = tot
+    for some, sem in sent:
+        pltpu.make_async_copy(some, some, sem).wait()
 
 
 def update_kernel(sol_v, res_v, dir_v, img_v, sums_v, osol_v, ores_v, odir_v):

time: 28.8 us -> 27.4 us (0.951)
  Pallas kernels: 27.9 us -> 26.6 us
    pallas_call x1, Pallas kernels: 25.6 us -> 24.3 us  [body(): pl.pallas_call(functools.partial(kernel, nb, nd, mo, rr, kl, two), out_sh...]
where the time goes in v3:
time: 27.4 us; the launch traced here: 27.2 us
  Pallas kernels  26.6 us (97%)
  between operations  0.64 us (2%)
    pallas_call x1, Pallas kernels, body(): pl.pallas_call(functools.partial(kernel, nb, nd, mo, rr, kl, two), out_sh...  24.3 us
    pallas_call x1, Pallas kernels, body(): pl.pallas_call(update_kernel, out_shape=(flat_shape,) * 3, in_specs=[vmem...  2.26 us

profile of v3, /device:TPU:0, one launch (start us, length us, event | category | flops | bytes accessed | tf_op | source)
XLA Modules:
  0.0 27.2 jit_solution(16040869912343010188)
XLA Ops:
  0.6 24.3 %cg_step.1 = (f32[528,128]{1,0:T(8,128)}, f32[8,128]{1,0:T(8,128)}) custom-call(f32[528,128]{1,0:T(8,128)} %bitcast.53, f32[528,128]{1,0:T(8,128)} %bitcast.55, bf16[1056,128]{1,0:T(8,128)(2,1)} %bitcast.58, f32[8,1024]{1,0:T(8,128)} %bitcast.60, f32[8,128]{1,0:T(8,128)} %bitcast.62, s32[1,32]{1,0:T(1,128)} %ids_v.1, s32[1,32]{1,0:T(1,128)} %ids_v.1, ...), custom_call_target="tpu_custom_call" | custom-call | tf_op jit(solution)/shard_map/cg_step/pallas_call | solution.py:432
  25.0 2.3 %cg_update.1 = (f32[528,128]{1,0:T(8,128)}, f32[528,128]{1,0:T(8,128)}, f32[528,128]{1,0:T(8,128)}) custom-call(f32[528,128]{1,0:T(8,128)} %bitcast.59, f32[528,128]{1,0:T(8,128)} %bitcast.54, f32[528,128]{1,0:T(8,128)} %bitcast.56, f32[528,128]{1,0:T(8,128)} %get-tuple-element.8.img_v, f32[8,128]{1,0:T(8,128)} %get-tuple-element.9.sums_v), custom_call_target="tpu_custom_call" | custom-call | tf_op jit(solution)/shard_map/cg_update/pallas_call | solution.py:447

commit v4 on v3

--- a/solution.py
+++ b/solution.py
@@ -67,10 +67,10 @@
 
 def kernel(
     nb, nd, mo, rr, kl, two, res_h, dir_h, leg_h, beam_v, prior_v, ids_s, ids_v, w_h, psi_v,
-    noise_s, band_s, table_h, back_h, img, sums_v,
+    noise_s, band_s, table_h, back_h, img_h, sums_v,
     res_v, dir_v, leg_v, legf, w_v, table_v, back_s, yhi, ylo, part, asend, arecv, coef, brecv,
-    tiles, basis, prod, sigs, filt, sadj, tt, adj, dsend, drecv, erecv, backf, gsend, grecv,
-    in_sem, b_sem, a_ss, a_rs, c_sem, d_ss, d_rs, e_ss, e_rs, g_ss, g_rs,
+    tiles, basis, prod, sigs, filt, sadj, tt, adj, dsend, drecv, erecv, backf, img, gsend, grecv,
+    in_sem, b_sem, a_ss, a_rs, c_sem, d_ss, d_rs, e_ss, e_rs, g_ss, g_rs, i_sem,
 ):
     n = nb * nd
     back_v = back_s if two else None
@@ -353,12 +353,15 @@
         ).start()
 
     loop(n - 1, g_send)
+    i_copy = pltpu.make_async_copy(img, img_h, i_sem)
+    i_copy.start()
     grecv[me] = gsend[...]
     wait_all(grecv, g_ss, g_rs)
     tot = grecv[0]
     for i in range(1, n):
         tot = tot + grecv[i]
     sums_v[...] = tot
+    i_copy.wait()
     for some, sem in sent:
         pltpu.make_async_copy(some, some, sem).wait()
 
@@ -422,9 +425,9 @@
         V((tiles_all * kl, TPIX), F32), V((kr, P_SIZE), F32),
         V((nb, kr, LANES), BF16), V((n, kr, LANES), BF16),
         V((2, kr, LANES), BF16), V((2, kr, LANES), F32),
-        V((8, LANES), F32), V((n, 8, LANES), F32),
+        V((frows, LANES), F32), V((8, LANES), F32), V((n, 8, LANES), F32),
         dma((6,)), dma((2,)), dma, dma, dma((2,)), dma, dma,
-        dma, dma, dma, dma,
+        dma, dma, dma, dma, dma,
     ]
     held = sum(
         math.prod(v.shape) * v.dtype.itemsize for v in scratch if hasattr(v, 'dtype') and getattr(v, 'memory_space', None) == V)
@@ -433,7 +436,7 @@
         functools.partial(kernel, nb, nd, mo, rr, kl, two),
         out_shape=(flat_shape, jax.ShapeDtypeStruct((8, LANES), F32)),
         in_specs=[any_spec] * 3 + [vmem, vmem, smem, vmem, any_spec, vmem, smem, smem, any_spec, any_spec],
-        out_specs=(vmem, vmem),
+        out_specs=(any_spec, vmem),
         scratch_shapes=scratch,
         compiler_params=pltpu.CompilerParams(
             collective_id=0, has_side_effects=True, vmem_limit_bytes=60 * 1024 * 1024

time: 27.4 us -> 27.3 us (level)
  no operation moved by 1% of the time
where the time goes in v4:
time: 27.3 us; the launch traced here: 27.1 us
  Pallas kernels  26.5 us (97%)
  between operations  0.64 us (2%)
    pallas_call x1, Pallas kernels, body(): pl.pallas_call(functools.partial(kernel, nb, nd, mo, rr, kl, two), out_sh...  24.2 us
    pallas_call x1, Pallas kernels, body(): pl.pallas_call(update_kernel, out_shape=(flat_shape,) * 3, in_specs=[vmem...  2.26 us

profile of v4, /device:TPU:0, one launch (start us, length us, event | category | flops | bytes accessed | tf_op | source)
XLA Modules:
  0.0 27.1 jit_solution(6692373692017729365)
XLA Ops:
  0.6 24.2 %cg_step.1 = (f32[528,128]{1,0:T(8,128)}, f32[8,128]{1,0:T(8,128)}) custom-call(f32[528,128]{1,0:T(8,128)} %bitcast.53, f32[528,128]{1,0:T(8,128)} %bitcast.55, bf16[1056,128]{1,0:T(8,128)(2,1)} %bitcast.58, f32[8,1024]{1,0:T(8,128)} %bitcast.60, f32[8,128]{1,0:T(8,128)} %bitcast.62, s32[1,32]{1,0:T(1,128)} %ids_v.1, s32[1,32]{1,0:T(1,128)} %ids_v.1, ...), custom_call_target="tpu_custom_call" | custom-call | tf_op jit(solution)/shard_map/cg_step/pallas_call | solution.py:435
  24.9 2.3 %cg_update.1 = (f32[528,128]{1,0:T(8,128)}, f32[528,128]{1,0:T(8,128)}, f32[528,128]{1,0:T(8,128)}) custom-call(f32[528,128]{1,0:T(8,128)} %bitcast.59, f32[528,128]{1,0:T(8,128)} %bitcast.54, f32[528,128]{1,0:T(8,128)} %bitcast.56, f32[528,128]{1,0:T(8,128)} %get-tuple-element.8.img_v, f32[8,128]{1,0:T(8,128)} %get-tuple-element.9.sums_v), custom_call_target="tpu_custom_call" | custom-call | tf_op jit(solution)/shard_map/cg_update/pallas_call | solution.py:450
